TPU v7x, 128 devices: a whole 4x4x4 slice. The times are simulated.
128 devices in a mesh: fsdp: 32 (over z, y_hi, x), tp: 4 (over y_lo, core).
Axes of the slice: x: 4, y: 4 (y_hi: 2, y_lo: 2; y = y_hi * 2 + y_lo), z: 4, core: 2. Of those that a mesh axis runs over, the one named last changes fastest.
Arguments:
- inputs: bfloat16 [4, 64, 2560], P(None, 'fsdp'), may hold values from -6 to 6
- norm_gain: bfloat16 [2, 2560], replicated, may hold values from 0.099609375 to 1.8984375
- old_wq: bfloat16 [2, 2560, 4096], P(None, None, 'tp'), may hold values from -0.125 to 0.125
- old_wk: bfloat16 [2, 2560, 512], P(None, None, 'tp'), may hold values from -0.125 to 0.125
- old_wv: bfloat16 [2, 2560, 512], P(None, None, 'tp'), may hold values from -0.125 to 0.125
- old_wo: bfloat16 [2, 2560, 4096], P(None, None, 'tp'), may hold values from -0.09375 to 0.09375
- new_wq: bfloat16 [2, 2560, 4096], P(None, ('fsdp', 'tp')), may hold values from -0.125 to 0.125
- new_wk: bfloat16 [2, 2560, 512], P(None, ('fsdp', 'tp')), may hold values from -0.125 to 0.125
- new_wv: bfloat16 [2, 2560, 512], P(None, ('fsdp', 'tp')), may hold values from -0.125 to 0.125
- new_wo: bfloat16 [2, 2560, 4096], P(None, ('fsdp', 'tp')), may hold values from -0.09375 to 0.09375
- cache_keys: bfloat16 [2, 64, 256, 512], P(None, 'fsdp', None, 'tp'), may hold values from -120 to 120
- cache_values: bfloat16 [2, 64, 256, 512], P(None, 'fsdp', None, 'tp'), may hold values from -6 to 6
- cache_lengths: int32 [64], P('fsdp'), may hold values from 1 to 256, as said below
- refresh_bound: int32 [4], replicated, may hold values from 0 to 2, as said below
Outputs:
- stream_out: float32 [4, 64, 2560], P(None, 'fsdp')
Inputs may be any that keep to these rules, and one draw needn't show every extreme that they name: `cache_lengths`: some row has exactly 256 live slots. `refresh_bound`: never falls from step to step; it is 2 at the last step.
All inputs are finite; a program needn't handle non-finite values.
Results may differ from a plain program's by a relative error of at most 0.015.
Values may be sent and summed in bfloat16 or wider, within the bound.
A program may use at most 384 MiB of HBM per device.

v0:
```python
import math

import jax
import jax.numpy as jnp
from jax import lax
from jax.sharding import PartitionSpec as P

D = 2560
HD = 128
QB = 128
LAYERS = 2
STEPS = 4
GROUPS = 4
REPLICAS = 32
WORLD = GROUPS * REPLICAS


def to_grid(values):
    magnitude = jnp.abs(values)
    exponent = jnp.floor(jnp.log2(jnp.maximum(magnitude, 2.0 ** (-6))))
    spacing = jnp.exp2(exponent - 3.0)
    return jnp.sign(values) * jnp.floor(magnitude / spacing + 0.5) * spacing


def partial_peaks(weight, row_start):
    layer_count, row_count, col_count = weight.shape
    col_peaks = jnp.max(
        jnp.abs(weight).reshape(layer_count, row_count, col_count // QB, QB), axis=3
    ).astype(jnp.float32)
    row_block = (row_start + jnp.arange(row_count)) // QB
    in_block = row_block[:, None] == jnp.arange(D // QB)[None, :]
    return jnp.max(jnp.where(in_block[None, :, :, None], col_peaks[:, :, None, :], 0.0), axis=1)


def refresh(weight, peak_table, row_start):
    layer_count, row_count, col_count = weight.shape
    scales = (peak_table + 1e-06) / 448.0
    row_block = (row_start + jnp.arange(row_count)) // QB
    scales = jnp.take(scales, row_block, axis=1)[..., None]
    blocked = weight.astype(jnp.float32).reshape(layer_count, row_count, col_count // QB, QB)
    coded = to_grid(blocked / scales)
    return (coded * scales).astype(jnp.bfloat16).reshape(layer_count, row_count, col_count)


def normed(hidden, gain):
    mean_square = jnp.mean(hidden * hidden, axis=-1, keepdims=True)
    return (hidden * lax.rsqrt(mean_square + 1e-06) * gain.astype(jnp.float32)).astype(jnp.bfloat16)


def attend(queries, cache_k, cache_v, step_k, step_v, lengths):
    rows = cache_k.shape[0]
    score_scale = 1.0 / math.sqrt(HD)
    query = queries.reshape(STEPS, rows, 8, HD)
    old = jnp.einsum("srgd,rcd->srgc", query, cache_k, preferred_element_type=jnp.float32)
    live = jnp.arange(cache_k.shape[1])[None, :] < lengths[:, None]
    old = jnp.where(live[None, :, None, :], old * score_scale, -1e30)
    new = jnp.einsum("srgd,urd->srgu", query, step_k, preferred_element_type=jnp.float32)
    seen = jnp.arange(STEPS)[None, :] <= jnp.arange(STEPS)[:, None]
    new = jnp.where(seen[:, None, None, :], new * score_scale, -1e30)
    peak = jnp.maximum(jnp.max(old, axis=3), jnp.max(new, axis=3))[..., None]
    prob_old = jnp.exp(old - peak)
    prob_new = jnp.exp(new - peak)
    total = jnp.sum(prob_old, axis=3) + jnp.sum(prob_new, axis=3)
    weighted = jnp.einsum(
        "srgc,rcd->srgd",
        prob_old.astype(jnp.bfloat16),
        cache_v,
        preferred_element_type=jnp.float32,
    )
    weighted = weighted + jnp.einsum(
        "srgu,urd->srgd",
        prob_new.astype(jnp.bfloat16),
        step_v,
        preferred_element_type=jnp.float32,
    )
    return (weighted / total[..., None]).astype(jnp.bfloat16).reshape(STEPS, rows, 8 * HD)


def on_device(
    inputs,
    norm_gain,
    old_wq,
    old_wk,
    old_wv,
    old_wo,
    new_wq,
    new_wk,
    new_wv,
    new_wo,
    cache_keys,
    cache_values,
    cache_lengths,
    refresh_bound,
):
    replica = lax.axis_index("fsdp")
    row_start = lax.axis_index(("fsdp", "tp")) * new_wq.shape[1]
    trained = jnp.concatenate([new_wq, new_wk, new_wv, new_wo], axis=2)
    peaks = lax.pmax(partial_peaks(trained, row_start), ("fsdp", "tp"))
    fresh = refresh(trained, peaks, row_start)
    fresh_q, fresh_k, fresh_v, fresh_o = jnp.split(fresh, (4096, 4608, 5120), axis=2)

    def by_destination(matrix):
        each = matrix.shape[2] // WORLD
        cut = matrix.reshape(LAYERS, 20, GROUPS, REPLICAS, each)
        return cut.transpose(3, 2, 0, 1, 4).reshape(WORLD, LAYERS, 20, each)

    moving = jnp.concatenate([by_destination(m) for m in (fresh_q, fresh_k, fresh_v)], axis=3)
    landed = lax.all_to_all(moving, ("fsdp", "tp"), split_axis=0, concat_axis=0, tiled=True)
    fresh_in = landed.transpose(1, 0, 2, 3).reshape(LAYERS, D, 40)
    moving = fresh_o.reshape(LAYERS, 20, GROUPS, 1024).transpose(2, 0, 1, 3)
    landed = lax.all_to_all(moving, "tp", split_axis=0, concat_axis=0, tiled=True)
    fresh_out = landed.transpose(1, 0, 2, 3).reshape(LAYERS, 80, 1024)

    def own_columns(matrix):
        each = matrix.shape[2] // REPLICAS
        return lax.dynamic_slice_in_dim(matrix, replica * each, each, 2)

    stale_in = jnp.concatenate([own_columns(m) for m in (old_wq, old_wk, old_wv)], axis=2)
    stale_out = lax.dynamic_slice_in_dim(old_wo, replica * 80, 80, 1)

    hidden = inputs.astype(jnp.float32)
    rows = hidden.shape[1]
    for layer in range(LAYERS):
        use_new = (layer < refresh_bound)[None, :, None, None]
        normed_x = normed(hidden, norm_gain[layer])
        everyone = lax.all_gather(normed_x, "fsdp", axis=0)
        both = jnp.concatenate([fresh_in[layer], stale_in[layer]], axis=1)
        product = jnp.einsum("fsrd,de->fsre", everyone, both, preferred_element_type=jnp.float32)
        product = product.astype(jnp.bfloat16)
        product = jnp.where(use_new, product[..., :40], product[..., 40:])
        mine = lax.all_to_all(product, "fsdp", split_axis=0, concat_axis=0, tiled=True)
        mine = mine.transpose(1, 2, 0, 3)
        queries = mine[..., :32].reshape(STEPS, rows, 1024)
        step_k = mine[..., 32:36].reshape(STEPS, rows, HD)
        step_v = mine[..., 36:].reshape(STEPS, rows, HD)
        attended = attend(
            queries, cache_keys[layer], cache_values[layer], step_k, step_v, cache_lengths
        )
        everyone = lax.all_gather(attended, "fsdp", axis=0)
        both = jnp.concatenate([fresh_out[layer], stale_out[layer]], axis=0)
        product = jnp.einsum("fsrd,ed->fsre", everyone, both, preferred_element_type=jnp.float32)
        product = jnp.where(use_new, product[..., :80], product[..., 80:])
        mine = lax.all_to_all(product, "fsdp", split_axis=0, concat_axis=0, tiled=True)
        mine = mine.transpose(1, 2, 0, 3).reshape(STEPS, rows, D)
        hidden = hidden + lax.psum(mine, "tp")
    return hidden


def solution(mesh):
    in_specs = (
        P(None, "fsdp", None),
        P(),
        P(None, None, "tp"),
        P(None, None, "tp"),
        P(None, None, "tp"),
        P(None, None, "tp"),
        P(None, ("fsdp", "tp"), None),
        P(None, ("fsdp", "tp"), None),
        P(None, ("fsdp", "tp"), None),
        P(None, ("fsdp", "tp"), None),
        P(None, "fsdp", None, "tp"),
        P(None, "fsdp", None, "tp"),
        P("fsdp"),
        P(),
    )
    out_specs = P(None, "fsdp", None)
    return jax.shard_map(
        on_device, mesh=mesh, in_specs=in_specs, out_specs=out_specs, check_vma=False
    )
```

profile of v0, /device:TPU:1, one launch (start us, length us, event | category | flops | bytes accessed | tf_op | source)
XLA Modules:
  0.0 583.9 jit_solution(18133777472324503225)
XLA Ops:
  14.3 68.9 %pmax.7 = f32[2,20,72]{2,0,1:T(2,128)S(1)} all-reduce(f32[2,20,72]{2,0,1:T(2,128)S(1)} %select_reduce_fusion), channel_id=1, replica_groups=mesh['fsdp'=32,'tp'=4] {'fsdp','tp'}, use_global_device_ids=true, to_apply=%region_3.4 | all-reduce | flops 2880 | bytes 23040 | tf_op jit(solution)/shard_map/pmax | solution.py:98
  85.3 7.0 %multiply_convert_fusion = bf16[2,20,9216]{2,0,1:T(2,128)(2,1)S(1)} fusion(f32[2,20,9216]{2,0,1:T(2,128)S(1)} %div.77, bf16[2,20,9216]{2,0,1:T(2,128)(2,1)} %copy-done), kind=kLoop, calls=%fused_computation.1 | loop fusion | flops 5898240 | bytes 2949120 | tf_op jit(solution)/shard_map/convert_element_type | solution.py:42
  94.8 2.6 copy.153
  98.6 4.6 copy.154
  103.2 2.5 pad_maximum_fusion
  105.7 1.3 copy.222
  107.1 2.9 reshape.285
  110.0 4.7 all-to-all-start
  115.7 3.6 constant_dynamic-slice_fusion
  119.3 1.7 constant_dynamic-slice_fusion.2
  121.0 1.8 copy.207
  125.0 1.8 dynamic-slice_bitcast_fusion
  128.0 4.3 all-to-all-start.2
  132.3 1.8 reshape.286
  135.0 7.6 %slice_reduce_fusion = (bf16[128,20,40]{2,1,0:T(8,128)(2,1)S(1)}, bf16[128,20,40]{2,1,0:T(8,128)(2,1)S(1)}) fusion(bf16[2,128,20,40]{3,0,2,1:T(2,128)(2,1)S(1)} %bitcast_bitcast_fusion), kind=kLoop, calls=%fused_computation.4 | loop fusion | bytes 819200 | tf_op jit(solution)/shard_map/slice | solution.py:127
  143.1 43.0 %all-gather.5.cloned.1.call-done = bf16[128,2,2560]{2,1,0:T(2,128)(2,1)} async-done(((bf16[4,2,2560]{2,1,0:T(2,128)(2,1)}), bf16[128,2,2560]{2,1,0:T(2,128)(2,1)}) %all-gather.5.cloned.1.call-update) | async-done | bytes 1310736 | tf_op jit(solution)/shard_map/all_gather | solution.py:126
  186.1 1.8 fusion.4
  188.9 4.6 all-to-all-start.1
  193.5 1.4 slice_reduce_fusion.2
  194.9 7.2 %all-to-all-done.1 = bf16[32,2,160]{2,1,0:T(2,128)(2,1)S(1)} async-done(((bf16[32,2,160]{2,1,0:T(2,128)(2,1)}), bf16[32,2,160]{2,1,0:T(2,128)(2,1)S(1)}, u32[]{:S(2)}, u32[]{:S(2)}) %all-to-all-start.1) | async-done | bytes 20512 | tf_op jit(solution)/shard_map/all_to_all | solution.py:131
  204.0 78.1 %all_gather.20 = bf16[32,4,2,1024]{3,1,2,0:T(4,128)(2,1)S(1)} all-gather(bf16[1,4,2,1024]{3,1,2,0:T(4,128)(2,1)S(1)} %all_gather_reshape.6), channel_id=1, replica_groups=mesh['fsdp'=32,'tp'=4] {'fsdp'}, dimensions={0}, use_global_device_ids=true | all-gather | bytes 540672 | tf_op jit(solution)/shard_map/all_gather | solution.py:139
  283.1 12.1 %all_to_all.30 = f32[32,4,2,80]{3,2,1,0:T(2,128)S(1)} all-to-all(f32[32,4,2,80]{3,2,1,0:T(2,128)S(1)} %copy.169), channel_id=1, replica_groups=mesh['fsdp'=32,'tp'=4] {'fsdp'}, dimensions={0} | all-to-all | bytes 163840 | tf_op jit(solution)/shard_map/all_to_all | solution.py:143
  296.0 49.9 %all-reduce.3.cloned.1.call-done = f32[4,2,2560]{2,1,0:T(2,128)} async-done(((f32[4,2,2560]{2,1,0:T(2,128)}), f32[4,2,2560]{2,1,0:T(2,128)}) %all-reduce.3.cloned.1.call-update) | async-done | bytes 81936 | tf_op jit(solution)/shard_map/psum | solution.py:145
  347.0 1.6 multiply_convert_fusion.1
  349.1 66.9 %all-gather.7.cloned.1.call-done = bf16[128,2,2560]{2,1,0:T(2,128)(2,1)} async-done(((bf16[4,2,2560]{2,1,0:T(2,128)(2,1)}), bf16[128,2,2560]{2,1,0:T(2,128)(2,1)}) %all-gather.7.cloned.1.call-update) | async-done | bytes 1310736 | tf_op jit(solution)/shard_map/all_gather | solution.py:126
  416.0 1.8 fusion.7
  418.8 4.3 all-to-all-start.4
  423.2 8.6 %all-to-all-done.4 = bf16[32,2,160]{2,1,0:T(2,128)(2,1)S(1)} async-done(((bf16[32,2,160]{2,1,0:T(2,128)(2,1)}), bf16[32,2,160]{2,1,0:T(2,128)(2,1)S(1)}, u32[]{:S(2)}, u32[]{:S(2)}) %all-to-all-start.4) | async-done | bytes 20512 | tf_op jit(solution)/shard_map/all_to_all | solution.py:131
  433.7 77.9 %all_gather.23 = bf16[32,4,2,1024]{3,1,2,0:T(4,128)(2,1)S(1)} all-gather(bf16[1,4,2,1024]{3,1,2,0:T(4,128)(2,1)S(1)} %all_gather_reshape.7), channel_id=1, replica_groups=mesh['fsdp'=32,'tp'=4] {'fsdp'}, dimensions={0}, use_global_device_ids=true | all-gather | bytes 540672 | tf_op jit(solution)/shard_map/all_gather | solution.py:139
  512.5 12.1 %all_to_all.31 = f32[32,4,2,80]{3,2,1,0:T(2,128)S(1)} all-to-all(f32[32,4,2,80]{3,2,1,0:T(2,128)S(1)} %copy.180), channel_id=1, replica_groups=mesh['fsdp'=32,'tp'=4] {'fsdp'}, dimensions={0} | all-to-all | bytes 163840 | tf_op jit(solution)/shard_map/all_to_all | solution.py:143
  525.5 50.1 %all-reduce.5.cloned.1.call-done = f32[4,2,2560]{2,1,0:T(2,128)} async-done(((f32[4,2,2560]{2,1,0:T(2,128)}), f32[4,2,2560]{2,1,0:T(2,128)}) %all-reduce.5.cloned.1.call-update) | async-done | bytes 81936 | tf_op jit(solution)/shard_map/psum | solution.py:145
  575.6 1.5 fusion.63
  (131 shorter events, 29.8 us)
Async XLA Ops:
  10.8 0.9 copy-start
  107.1 7.6 %copy-start.8 = (bf16[2,2560]{1,0:T(2,128)(2,1)S(1)}, bf16[2,2560]{1,0:T(2,128)(2,1)}, u32[]{:S(2)}) copy-start(bf16[2,2560]{1,0:T(2,128)(2,1)} %param.15) | copy-start | bytes 30724
  107.1 7.7 %copy-start.1 = (bf16[4,2,2560]{2,1,0:T(2,128)(2,1)S(1)}, bf16[4,2,2560]{2,1,0:T(2,128)(2,1)}, u32[]{:S(2)}) copy-start(bf16[4,2,2560]{2,1,0:T(2,128)(2,1)} %param.14) | copy-start | bytes 122884
  110.0 18.1 %all-to-all-start = ((bf16[128,2,800]{2,1,0:T(2,128)(2,1)}), bf16[128,2,800]{2,1,0:T(2,128)(2,1)S(1)}, u32[]{:S(2)}, u32[]{:S(2)}) async-start(bf16[128,2,800]{2,1,0:T(2,128)(2,1)} %reshape.285), calls=%async_computation | async-start | bytes 917504 | tf_op jit(solution)/shard_map/all_to_all | solution.py:108
  114.7 71.5 %all-gather.5.cloned.1.call-start = ((), (), s32[]{:S(2)}) async-start(), calls=%async_computation.8 | async-start | bytes 1351680 | tf_op jit(solution)/shard_map/all_gather | solution.py:126
  125.0 2.5 copy-start.9
  125.0 2.5 copy-start.10
  128.0 60.9 %all-to-all-start.2 = ((bf16[4,2,20,1024]{3,1,2,0:T(2,128)(2,1)}), bf16[4,2,20,1024]{3,1,2,0:T(2,128)(2,1)S(1)}, u32[]{:S(2)}, u32[]{:S(2)}) async-start(bf16[4,2,20,1024]{3,1,2,0:T(2,128)(2,1)} %copy.167), calls=%async_computation.2 | async-start | bytes 655360 | tf_op jit(solution)/shard_map/all_to_all | solution.py:111
  142.6 43.5 %copy-start.5 = (bf16[2560,40]{0,1:T(8,128)(2,1)S(1)}, bf16[2560,40]{0,1:T(8,128)(2,1)}, u32[]{:S(2)}) copy-start(bf16[2560,40]{0,1:T(8,128)(2,1)} %get-tuple-element.18) | copy-start | bytes 614404
  188.1 14.9 %copy-start.4 = (bf16[2,2,256,128]{3,2,1,0:T(8,128)(2,1)S(1)}, bf16[2,2,256,128]{3,2,1,0:T(8,128)(2,1)}, u32[]{:S(2)}) copy-start(bf16[2,2,256,128]{3,2,1,0:T(8,128)(2,1)} %param.24) | copy-start | bytes 786436
  188.9 13.3 %all-to-all-start.1 = ((bf16[32,2,160]{2,1,0:T(2,128)(2,1)}), bf16[32,2,160]{2,1,0:T(2,128)(2,1)S(1)}, u32[]{:S(2)}, u32[]{:S(2)}) async-start(bf16[32,2,160]{2,1,0:T(2,128)(2,1)} %reshape.287), calls=%async_computation.1 | async-start | bytes 65536 | tf_op jit(solution)/shard_map/all_to_all | solution.py:131
  193.5 10.0 %copy-start.3 = (bf16[2,2,256,128]{3,2,1,0:T(8,128)(2,1)S(1)}, bf16[2,2,256,128]{3,2,1,0:T(8,128)(2,1)}, u32[]{:S(2)}) copy-start(bf16[2,2,256,128]{3,2,1,0:T(8,128)(2,1)} %param.25) | copy-start | bytes 786436
  193.5 152.5 %all-reduce.3.cloned.1.call-start = ((), (), s32[]{:S(2)}) async-start(), calls=%async_computation.6 | async-start | bytes 163840 | tf_op jit(solution)/shard_map/psum | solution.py:145
  194.9 87.2 %copy-start.7 = (bf16[80,1024]{1,0:T(8,128)(2,1)S(1)}, bf16[80,1024]{1,0:T(8,128)(2,1)}, u32[]{:S(2)}) copy-start(bf16[80,1024]{1,0:T(8,128)(2,1)} %get-tuple-element.12) | copy-start | bytes 491524
  296.0 120.0 %all-gather.7.cloned.1.call-start = ((), (), s32[]{:S(2)}) async-start(), calls=%async_computation.9 | async-start | bytes 1351680 | tf_op jit(solution)/shard_map/all_gather | solution.py:126
  418.8 13.1 %all-to-all-start.4 = ((bf16[32,2,160]{2,1,0:T(2,128)(2,1)}), bf16[32,2,160]{2,1,0:T(2,128)(2,1)S(1)}, u32[]{:S(2)}, u32[]{:S(2)}) async-start(bf16[32,2,160]{2,1,0:T(2,128)(2,1)} %reshape.289), calls=%async_computation.4 | async-start | bytes 65536 | tf_op jit(solution)/shard_map/all_to_all | solution.py:131
  423.1 152.5 %all-reduce.5.cloned.1.call-start = ((), (), s32[]{:S(2)}) async-start(), calls=%async_computation.7 | async-start | bytes 163840 | tf_op jit(solution)/shard_map/psum | solution.py:145
  423.2 88.4 %copy-start.6 = (bf16[80,1024]{1,0:T(8,128)(2,1)S(1)}, bf16[80,1024]{1,0:T(8,128)(2,1)}, u32[]{:S(2)}) copy-start(bf16[80,1024]{1,0:T(8,128)(2,1)} %get-tuple-element.11) | copy-start | bytes 491524
  511.6 64.0 %copy-start.2 = (f32[4,2,2560]{2,1,0:T(2,128)S(1)}, f32[4,2,2560]{2,1,0:T(2,128)}, u32[]{:S(2)}) copy-start(f32[4,2,2560]{2,1,0:T(2,128)} %all-reduce.3.cloned.1.call-done) | copy-start | bytes 245764
Sparse Core Ops, SparseCore 0:
  118.6 67.5 all-gather.4
  296.1 49.7 all-reduce.2
  349.5 66.4 all-gather.6
  525.6 49.9 all-reduce.4
where the time goes:
time: 590 us; the launch traced here: 584 us
  blocking collectives  249 us (42%)
  waiting for transfers between devices  226 us (38%)
  local copies, waits for them, and re-layouts  51.8 us (9%)
  other arithmetic  18 us (3%)
  starting transfers between devices  18 us (3%)
  between operations  14 us (2%)
  matrix products  6.71 us (1%)
    all_gather x2, blocking collectives, on_device(): everyone = lax.all_gather(attended, 'fsdp', axis=0)  156 us
    all_gather x2, waiting for transfers between devices, on_device(): everyone = lax.all_gather(normed_x, 'fsdp', axis=0)  110 us
    psum x2, waiting for transfers between devices, on_device(): hidden = hidden + lax.psum(mine, 'tp')  100 us
    pmax x1, blocking collectives, on_device(): peaks = lax.pmax(partial_peaks(trained, row_start), ('fsdp', 'tp'))  68.9 us
    all_to_all x2, blocking collectives, on_device(): lax.all_to_all(product, 'fsdp', split_axis=0, concat_axis=0, tiled=True)  24.1 us
    all_to_all x2, waiting for transfers between devices, on_device(): lax.all_to_all(product, 'fsdp', split_axis=0, concat_axis=0, tiled=True)  15.9 us
    unnamed x34, local copies, waits for them, and re-layouts  12.9 us
  transfers between devices with their start and end apart: 8, of which 7 were waited for; matrix products, arithmetic and copies ran while one was open for 5% of the time, Pallas kernels for 0%

commit v1 on v0

v1 whole, which is shorter than its diff:
```python
import functools
import math

import jax
import jax.numpy as jnp
from jax import lax
from jax.experimental import pallas as pl
from jax.experimental.pallas import tpu as pltpu
from jax.sharding import PartitionSpec as P

MESH = pl.DeviceIdType.MESH
D = 2560
HD = 128
STEPS = 4
OWNERS = 32
KEEP = 20
PART = 640
HALF = 512
ROWS = 256


def use_new_rows(bound_ref, layer, row_count):
    step = lax.rem(lax.broadcasted_iota(jnp.int32, (row_count, 1), 0), 8) // 2
    bound = jnp.where(
        step == 0,
        bound_ref[0],
        jnp.where(step == 1, bound_ref[1], jnp.where(step == 2, bound_ref[2], bound_ref[3])),
    )
    return layer < bound


def refresh_block(block):
    peak = jnp.max(jnp.abs(block), axis=(0, 1), keepdims=True)
    scale = (peak + 1e-06) / 448.0
    value = block / scale
    magnitude = jnp.abs(value)
    exponent = jnp.floor(jnp.log2(jnp.maximum(magnitude, 2.0 ** (-6))))
    coded = jnp.floor(magnitude * jnp.exp2(3.0 - exponent) + 0.5) * jnp.exp2(exponent - 3.0)
    coded = jnp.where(value < 0.0, -coded, coded).astype(jnp.bfloat16).astype(jnp.float32)
    return (coded * scale).astype(jnp.bfloat16)


def attend(sums, keys, values, length_ref):
    score_scale = 1.0 / math.sqrt(HD)
    queries = jnp.concatenate(
        [sums[g][:, HD * h : HD * h + HD] for g in range(2) for h in range(4)], axis=0
    ).astype(jnp.bfloat16)
    step_k = sums[0][:, HALF:PART].astype(jnp.bfloat16)
    step_v = sums[1][:, HALF:PART].astype(jnp.bfloat16)
    nt = (((1,), (1,)), ((), ()))
    old = lax.dot_general(queries, keys, nt, preferred_element_type=jnp.float32) * score_scale
    new = lax.dot_general(queries, step_k, nt, preferred_element_type=jnp.float32) * score_scale
    row = lax.broadcasted_iota(jnp.int32, (64, 512), 0)
    col = lax.broadcasted_iota(jnp.int32, (64, 512), 1)
    same = lax.rem(row, 2) == col // 256
    length = jnp.where(col // 256 == 0, length_ref[0], length_ref[1])
    old = jnp.where(same & (lax.rem(col, 256) < length), old, -1e30)
    row = lax.broadcasted_iota(jnp.int32, (64, 8), 0)
    col = lax.broadcasted_iota(jnp.int32, (64, 8), 1)
    same = lax.rem(row, 2) == lax.rem(col, 2)
    new = jnp.where(same & (col // 2 <= lax.rem(row, 8) // 2), new, -1e30)
    peak = jnp.maximum(
        jnp.max(old, axis=1, keepdims=True), jnp.max(new, axis=1, keepdims=True)
    )
    old = jnp.exp(old - peak)
    new = jnp.exp(new - peak)
    total = jnp.sum(old, axis=1, keepdims=True) + jnp.sum(new, axis=1, keepdims=True)
    mixed = jnp.dot(old.astype(jnp.bfloat16), values, preferred_element_type=jnp.float32)
    mixed = mixed + jnp.dot(new.astype(jnp.bfloat16), step_v, preferred_element_type=jnp.float32)
    return (mixed / total).astype(jnp.bfloat16)


def kernel(
    x0_ref,
    xr_ref,
    gain_ref,
    length_ref,
    bound_ref,
    old_wq,
    old_wk,
    old_wv,
    old_wo,
    new_wq,
    new_wk,
    new_wv,
    new_wo,
    cache_k,
    cache_v,
    out_ref,
    slabs,
    raw,
    fresh,
    stale,
    keys,
    values,
    x_land,
    r_land,
    product,
    b0_land,
    b1_land,
    att,
    d_land,
    e_land,
    ag_land,
    h_keep,
    h_land,
    f_land,
    f_keep,
    o_land,
    w_send,
    x_send,
    r_send,
    b_send,
    d_send,
    e_send,
    ag_send,
    h_send,
    f_send,
    o_send,
    w_recv,
    own_sem,
    local_sem,
    x_recv,
    r_recv,
    b_recv,
    d_recv,
    e_recv,
    ag_recv,
    h_recv,
    f_recv,
    o_recv,
):
    f = lax.axis_index("fsdp")
    t = lax.axis_index("tp")
    z = f // 8
    n = lax.rem(f, 8)
    g = n // 4
    role = lax.rem(lax.rem(n, 4) + 2 * lax.rem(t, 2), 4)
    lane = n * 4 + t
    slot = 4 * g + t

    def holder(plane, kind, group, half):
        return plane * 8 + half * 4 + lax.rem(kind + 2 * lax.rem(group, 2), 4)

    def remote(src, dst, send_sem, recv_sem, target):
        return pltpu.make_async_remote_copy(
            src_ref=src,
            dst_ref=dst,
            send_sem=send_sem,
            recv_sem=recv_sem,
            device_id=target,
            device_id_type=MESH,
        )

    def loop(count, body):
        def step(i, carry):
            body(i)
            return carry

        lax.fori_loop(0, count, step, 0)

    def taken(ref, sem):
        pltpu.make_async_copy(ref, ref, sem).wait()

    def weight_copies(kind, i):
        group, half = lax.rem(i, 4), i // 4
        layer = kind // 2
        target = (holder(z, kind, group, half), group)
        mine = (target[0] == f) & (group == t)
        columns = pl.ds(pl.multiple_of(group * 1024 + half * 512, 512), HALF)
        narrow = pl.ds(pl.multiple_of(group * HD, HD), HD)
        wide_to = slabs.at[lane, :, pl.ds(0, HALF)]
        narrow_to = slabs.at[lane, :, pl.ds(HALF, HD)]
        if kind % 2 == 0:
            pieces = (
                (None, new_wq.at[layer, :, columns], wide_to, 0),
                (half == 0, new_wk.at[layer, :, narrow], narrow_to, 1),
                (half == 1, new_wv.at[layer, :, narrow], narrow_to, 1),
            )
        else:
            pieces = ((None, new_wo.at[layer, :, columns], wide_to, 0),)
        return target, mine, pieces

    def send_weights(kind):
        def one(i):
            target, mine, pieces = weight_copies(kind, i)
            for cond, src, dst, k in pieces:
                here = mine if cond is None else mine & cond
                there = jnp.logical_not(mine) if cond is None else jnp.logical_not(mine) & cond

                @pl.when(there)
                def _():
                    remote(src, dst, w_send.at[kind, i, k], w_recv, target).start()

                @pl.when(here)
                def _():
                    pltpu.make_async_copy(src, dst, own_sem.at[k]).start()

        loop(8, one)

    def sent_weights(kind):
        def one(i):
            target, mine, pieces = weight_copies(kind, i)
            for cond, src, dst, k in pieces:
                there = jnp.logical_not(mine) if cond is None else jnp.logical_not(mine) & cond

                @pl.when(there)
                def _():
                    remote(src, dst, w_send.at[kind, i, k], w_recv, target).wait_send()

        loop(8, one)

    def x_copy(i):
        plane, half = i // 2, lax.rem(i, 2)
        target = (holder(plane, 0, t, half), t)
        src = x0_ref.at[:, pl.ds(pl.multiple_of(plane * PART, HD), PART)]
        copy = remote(src, x_land.at[f], x_send.at[i], x_recv, target)
        return target[0] != f, copy

    def r_copy(i):
        group = lax.rem(f // 4, 4)
        half = f // 16
        target = (holder(i, 2, group, half), group)
        src = xr_ref.at[:, pl.ds(pl.multiple_of(i * PART, HD), PART)]
        copy = remote(src, r_land.at[lax.rem(f, 4)], r_send.at[i], r_recv, target)
        return (group == t) & (target[0] != f), copy

    def b_copy(land, width, layer, i):
        src = product.at[i, :, pl.ds(0, width)]
        copy = remote(src, land.at[2 * z + g], b_send.at[i], b_recv.at[layer], (i, t))
        return i != f, copy

    def d_copy(layer, i):
        plane, half = i // 2, lax.rem(i, 2)
        target = (holder(plane, 2 * layer + 1, t, half), t)
        copy = remote(
            att.at[layer, half],
            d_land.at[layer, f],
            d_send.at[layer, i],
            d_recv.at[layer],
            target,
        )
        return target[0] != f, copy

    def e_copy(i):
        group, half = lax.rem(i, 4), i // 4
        target = (holder(z, 2, group, half), group)
        src = product.at[pl.ds(4 * i, 4), :, pl.ds(0, PART)]
        return remote(src, e_land.at[slot], e_send.at[i], e_recv, target)

    def ag_copy(i):
        group, half = lax.rem(i, 4), i // 4
        target = (holder(z, 2, group, half), group)
        copy = remote(ag_land.at[slot], ag_land.at[slot], ag_send.at[i], ag_recv, target)
        return i != slot, copy

    def h_copy(i):
        row_of = 4 * slot + i
        target = (z * 8 + lax.rem(row_of, 8), row_of // 8)
        copy = remote(h_keep.at[i], h_land, h_send.at[i], h_recv, target)
        return (target[0] != f) | (target[1] != t), copy

    def f_copy(i):
        target = (z * 8 + lax.rem(i, 8), i // 8)
        src = product.at[i, :, pl.ds(0, PART)]
        copy = remote(src, f_land.at[slot], f_send.at[i], f_recv, target)
        return (target[0] != f) | (target[1] != t), copy

    def o_copy(i):
        target = (8 * t + n, i)
        copy = remote(f_keep, o_land.at[z], o_send.at[i], o_recv, target)
        return (target[0] != f) | (target[1] != t), copy

    def start_all(count, make):
        def one(i):
            cond, copy = make(i)
            pl.when(cond)(copy.start)

        loop(count, one)

    def sent_all(count, make):
        def one(i):
            cond, copy = make(i)
            pl.when(cond)(copy.wait_send)

        loop(count, one)

    barrier = pltpu.get_barrier_semaphore()

    def greet(target):
        pl.semaphore_signal(barrier, inc=1, device_id=target, device_id_type=MESH)

    def greet_plane(i):
        other = lax.rem(lane + 1 + i, 32)
        greet((z * 8 + other // 4, lax.rem(other, 4)))

    def greet_group(i):
        greet((lax.rem(z + 1 + i // 8, 4) * 8 + lax.rem(i, 8), t))

    def greet_line(i):
        greet((lax.rem(z + 1 + i // 3, 4) * 8 + n, lax.rem(t + 1 + lax.rem(i, 3), 4)))

    loop(31, greet_plane)
    loop(24, greet_group)
    loop(9, greet_line)

    rows = pl.ds(pl.multiple_of(z * PART, HD), PART)
    half_cols = pl.ds(pl.multiple_of(g * HALF, HALF), HALF)

    def stale_copies(act):
        for kind in range(4):
            layer = kind // 2

            @pl.when(role == kind)
            def _():
                wide = old_wq if kind % 2 == 0 else old_wo
                act(
                    pltpu.make_async_copy(
                        wide.at[layer, rows, half_cols],
                        stale.at[:, pl.ds(0, HALF)],
                        local_sem.at[0],
                    )
                )
                if kind % 2 == 0:
                    for half, narrow in enumerate((old_wk, old_wv)):

                        @pl.when(g == half)
                        def _():
                            act(
                                pltpu.make_async_copy(
                                    narrow.at[layer, rows, :],
                                    stale.at[:, pl.ds(HALF, HD)],
                                    local_sem.at[1],
                                )
                            )

    stale_copies(lambda copy: copy.start())
    key_copy = pltpu.make_async_copy(cache_k, keys, local_sem.at[2])
    value_copy = pltpu.make_async_copy(cache_v, values, local_sem.at[3])
    key_copy.start()
    value_copy.start()

    pl.semaphore_wait(barrier, 64)

    send_weights(0)
    start_all(8, x_copy)

    @pl.when(role == 0)
    def _():
        x_land[f] = x0_ref[:, pl.ds(pl.multiple_of(z * PART, HD), PART)]

    send_weights(1)
    start_all(4, r_copy)

    @pl.when((role == 2) & (lax.rem(f // 4, 4) == t) & (f // 16 == g))
    def _():
        r_land[lax.rem(f, 4)] = xr_ref[:, pl.ds(pl.multiple_of(z * PART, HD), PART)]

    send_weights(2)
    send_weights(3)

    def prepare(width):
        used = pl.ds(0, width)
        taken(slabs.at[pl.ds(0, 31), :, used], w_recv)
        taken(slabs.at[0, :, pl.ds(0, HALF)], own_sem.at[0])
        if width > HALF:
            taken(slabs.at[0, :, pl.ds(HALF, HD)], own_sem.at[1])

        def pair(i):
            both = [slabs[2 * i + j, :, 0:width].astype(jnp.float32) for j in range(2)]
            raw[pl.ds(pl.multiple_of(40 * i, 8), 40), 0:width] = jnp.concatenate(both, axis=0)

        loop(16, pair)

        def block_row(i):
            at = pl.ds(pl.multiple_of(i * HD, HD), HD)
            for c in range(width // HD):
                cols = slice(c * HD, c * HD + HD)
                fresh[at, cols] = refresh_block(raw[at, cols])

        loop(5, block_row)
        stale_copies(lambda copy: copy.wait())

    def project(x, layer):
        chosen = use_new_rows(bound_ref, layer, ROWS)
        new = jnp.dot(x, fresh[...], preferred_element_type=jnp.float32)
        old = jnp.dot(x, stale[...], preferred_element_type=jnp.float32)
        product[:, :, 0:PART] = jnp.where(chosen, new, old).reshape(OWNERS, 8, PART)

    def out_project(layer):
        @pl.when(role == 2 * layer + 1)
        def _():
            d_land[layer, f] = att[layer, g]
            taken(d_land.at[layer, pl.ds(0, 31)], d_recv.at[layer])

        landed = d_land[layer].astype(jnp.float32)
        x = jnp.concatenate(
            [landed[:, 8 * h : 8 * h + 8, :].reshape(ROWS, HD) for h in range(4)], axis=1
        ).astype(jnp.bfloat16)
        chosen = use_new_rows(bound_ref, layer, ROWS)
        nt = (((1,), (1,)), ((), ()))
        new = lax.dot_general(x, fresh[:, 0:HALF], nt, preferred_element_type=jnp.float32)
        old = lax.dot_general(x, stale[:, 0:HALF], nt, preferred_element_type=jnp.float32)
        product[:, :, 0:PART] = jnp.where(chosen, new, old).reshape(OWNERS, 8, PART)

    def attention(layer, land, width):
        @pl.when(role == 2 * layer)
        def _():
            land[2 * z + g] = product[f, :, 0:width]
            taken(land.at[pl.ds(0, 7)], b_recv.at[layer])

        @pl.when(role != 2 * layer)
        def _():
            taken(land, b_recv.at[layer])

        sums = [sum(land[2 * plane + half] for plane in range(4)) for half in range(2)]
        if width > PART:
            inverse = lax.rsqrt(sums[0][:, PART : PART + 1] / D + 1e-06)
            sums = [part * inverse for part in sums]
        mixed = attend(
            sums, keys[layer].reshape(512, HD), values[layer].reshape(512, HD), length_ref
        )
        att[layer] = mixed.reshape(2, 32, HD)
        start_all(8, functools.partial(d_copy, layer))

    @pl.when(role == 0)
    def _():
        prepare(PART)
        taken(x_land.at[pl.ds(0, 31)], x_recv)
        project(x_land[...].reshape(ROWS, PART).astype(jnp.bfloat16), 0)
        start_all(OWNERS, functools.partial(b_copy, b0_land, PART, 0))

    @pl.when(role == 1)
    def _():
        prepare(HALF)

    key_copy.wait()
    value_copy.wait()
    attention(0, b0_land, PART)

    @pl.when(role == 1)
    def _():
        out_project(0)
        loop(8, lambda i: e_copy(i).start())

    @pl.when(role == 2)
    def _():
        prepare(PART)
        own_rows = (slot // 4 == f // 16) & (lax.rem(slot, 4) == lax.rem(f // 4, 4))

        @pl.when(own_rows)
        def _():
            taken(r_land.at[pl.ds(0, 3)], r_recv)

        @pl.when(jnp.logical_not(own_rows))
        def _():
            taken(r_land, r_recv)

        taken(e_land, e_recv)
        hidden = r_land[...]
        for other in range(8):
            hidden = hidden + e_land[other]
        h_keep[...] = hidden
        hidden = hidden.reshape(32, PART)
        square = jnp.sum(hidden * hidden, axis=1, keepdims=True)
        gain = gain_ref[:, pl.ds(pl.multiple_of(z * PART, HD), PART)]
        high = square.astype(jnp.bfloat16).astype(jnp.float32)
        first = lax.broadcasted_iota(jnp.int32, (32, HD), 1) < 64
        ag_land[slot, :, 0:PART] = (hidden * gain).astype(jnp.bfloat16)
        ag_land[slot, :, PART : PART + HD] = jnp.where(first, high, square - high).astype(
            jnp.bfloat16
        )
        start_all(8, ag_copy)
        start_all(4, h_copy)

        @pl.when(2 * t + g == slot)
        def _():
            h_land[...] = h_keep[lax.rem(n, 4)]

        taken(ag_land.at[pl.ds(0, 7)], ag_recv)
        everyone = ag_land[...].reshape(ROWS, PART + HD)
        project(everyone[:, 0:PART], 1)
        parts = everyone[:, PART : PART + HD].astype(jnp.float32)
        squares = parts[:, 0:1] + parts[:, 64:65]
        product[:, :, PART : PART + HD] = jnp.broadcast_to(squares, (ROWS, HD)).reshape(
            OWNERS, 8, HD
        )
        start_all(OWNERS, functools.partial(b_copy, b1_land, PART + HD, 1))

    @pl.when(role == 3)
    def _():
        prepare(HALF)

    attention(1, b1_land, PART + HD)

    @pl.when(role == 3)
    def _():
        out_project(1)
        start_all(OWNERS, f_copy)
        f_land[slot] = product[8 * t + n, :, 0:PART]
        taken(f_land.at[pl.ds(0, 7)], f_recv)

    @pl.when(role != 3)
    def _():
        taken(f_land, f_recv)

    @pl.when(jnp.logical_not((role == 2) & (2 * t + g == slot)))
    def _():
        taken(h_land, h_recv)

    final = h_land[...]
    for other in range(8):
        final = final + f_land[other]
    f_keep[...] = final
    start_all(4, o_copy)

    @pl.when(z == t)
    def _():
        o_land[z] = final
        taken(o_land.at[pl.ds(0, 3)], o_recv)

    @pl.when(z != t)
    def _():
        taken(o_land, o_recv)

    for plane in range(4):
        out_ref[:, plane * PART : plane * PART + PART] = o_land[plane]

    for kind in range(4):
        sent_weights(kind)
    sent_all(8, x_copy)
    sent_all(4, r_copy)
    sent_all(8, functools.partial(d_copy, 0))
    sent_all(8, functools.partial(d_copy, 1))
    sent_all(4, o_copy)

    @pl.when(role == 0)
    def _():
        sent_all(OWNERS, functools.partial(b_copy, b0_land, PART, 0))

    @pl.when(role == 1)
    def _():
        loop(8, lambda i: e_copy(i).wait_send())

    @pl.when(role == 2)
    def _():
        sent_all(8, ag_copy)
        sent_all(4, h_copy)
        sent_all(OWNERS, functools.partial(b_copy, b1_land, PART + HD, 1))

    @pl.when(role == 3)
    def _():
        sent_all(OWNERS, f_copy)


def normed(hidden, gain):
    mean_square = jnp.mean(hidden * hidden, axis=-1, keepdims=True)
    return (hidden * lax.rsqrt(mean_square + 1e-06) * gain.astype(jnp.float32)).astype(jnp.bfloat16)


def on_device(
    inputs,
    norm_gain,
    old_wq,
    old_wk,
    old_wv,
    old_wo,
    new_wq,
    new_wk,
    new_wv,
    new_wo,
    cache_keys,
    cache_values,
    cache_lengths,
    refresh_bound,
):
    entering = inputs.astype(jnp.float32).reshape(8, D)
    first = normed(entering, norm_gain[0]).astype(jnp.float32)
    gain = norm_gain[1:2].astype(jnp.float32)
    vmem = pl.BlockSpec(memory_space=pltpu.VMEM)
    smem = pl.BlockSpec(memory_space=pltpu.SMEM)
    hbm = pl.BlockSpec(memory_space=pl.ANY)
    f32, bf16 = jnp.float32, jnp.bfloat16
    dma = pltpu.SemaphoreType.DMA
    out = pl.pallas_call(
        kernel,
        out_shape=jax.ShapeDtypeStruct((8, D), f32),
        in_specs=[vmem] * 3 + [smem] * 2 + [hbm] * 10,
        out_specs=vmem,
        scratch_shapes=[
            pltpu.VMEM((32, KEEP, PART), bf16),
            pltpu.VMEM((PART, PART), f32),
            pltpu.VMEM((PART, PART), bf16),
            pltpu.VMEM((PART, PART), bf16),
            pltpu.VMEM((2, 2, 256, HD), bf16),
            pltpu.VMEM((2, 2, 256, HD), bf16),
            pltpu.VMEM((OWNERS, 8, PART), f32),
            pltpu.VMEM((4, 8, PART), f32),
            pltpu.VMEM((OWNERS, 8, PART + HD), f32),
            pltpu.VMEM((8, 8, PART), f32),
            pltpu.VMEM((8, 8, PART + HD), f32),
            pltpu.VMEM((2, 2, 32, HD), bf16),
            pltpu.VMEM((2, OWNERS, 32, HD), bf16),
            pltpu.VMEM((8, 4, 8, PART), f32),
            pltpu.VMEM((8, 32, PART + HD), bf16),
            pltpu.VMEM((4, 8, PART), f32),
            pltpu.VMEM((8, PART), f32),
            pltpu.VMEM((8, 8, PART), f32),
            pltpu.VMEM((8, PART), f32),
            pltpu.VMEM((4, 8, PART), f32),
            dma((4, 8, 2)),
            dma((8,)),
            dma((4,)),
            dma((OWNERS,)),
            dma((2, 8)),
            dma((8,)),
            dma((8,)),
            dma((4,)),
            dma((OWNERS,)),
            dma((4,)),
            dma,
            dma((2,)),
            dma((4,)),
            dma,
            dma,
            dma((2,)),
            dma((2,)),
            dma,
            dma,
            dma,
            dma,
            dma,
        ],
        compiler_params=pltpu.CompilerParams(
            collective_id=0, has_side_effects=True, vmem_limit_bytes=40 * 1024 * 1024
        ),
    )(
        first,
        entering,
        gain,
        cache_lengths,
        refresh_bound,
        old_wq,
        old_wk,
        old_wv,
        old_wo,
        new_wq,
        new_wk,
        new_wv,
        new_wo,
        cache_keys,
        cache_values,
    )
    return out.reshape(STEPS, 2, D)


def solution(mesh):
    in_specs = (
        P(None, "fsdp", None),
        P(),
        P(None, None, "tp"),
        P(None, None, "tp"),
        P(None, None, "tp"),
        P(None, None, "tp"),
        P(None, ("fsdp", "tp"), None),
        P(None, ("fsdp", "tp"), None),
        P(None, ("fsdp", "tp"), None),
        P(None, ("fsdp", "tp"), None),
        P(None, "fsdp", None, "tp"),
        P(None, "fsdp", None, "tp"),
        P("fsdp"),
        P(),
    )
    out_specs = P(None, "fsdp", None)
    return jax.shard_map(
        on_device, mesh=mesh, in_specs=in_specs, out_specs=out_specs, check_vma=False
    )
```

time: 590 us -> 103 us (0.17)
  blocking collectives: 249 us -> 0 us
  waiting for transfers between devices: 226 us -> 0 us
  Pallas kernels: 0 us -> 88.3 us
  local copies, waits for them, and re-layouts: 51.8 us -> 11.3 us
  starting transfers between devices: 18 us -> 0 us
  other arithmetic: 18 us -> 2.45 us
  between operations: 14 us -> 0.04 us
  matrix products: 6.71 us -> 0 us
    all_gather x2 -> x0, blocking collectives: 156 us -> none  [on_device(): everyone = lax.all_gather(attended, 'fsdp', axis=0)]
    all_gather x2 -> x0, waiting for transfers between devices: 110 us -> none  [on_device(): everyone = lax.all_gather(normed_x, 'fsdp', axis=0)]
    psum x2 -> x0, waiting for transfers between devices: 100 us -> none  [on_device(): hidden = hidden + lax.psum(mine, 'tp')]
    pallas_call x0 -> x1, Pallas kernels: none -> 88.3 us  [on_device(): pl.pallas_call(kernel, out_shape=jax.ShapeDtypeStruct((8, D), f32), in_sp...]
    pmax x1 -> x0, blocking collectives: 68.9 us -> none  [on_device(): peaks = lax.pmax(partial_peaks(trained, row_start), ('fsdp', 'tp'))]
    all_to_all x2 -> x0, blocking collectives: 24.1 us -> none  [on_device(): lax.all_to_all(product, 'fsdp', split_axis=0, concat_axis=0, tiled=True)]
    all_to_all x4 -> x0, starting transfers between devices: 17.8 us -> none  [the longest x2 8.9 us: on_device(): lax.all_to_all(product, 'fsdp', split_axis=0, concat_axis=0, tiled=True)]
    all_to_all x4 -> x0, waiting for transfers between devices: 16.3 us -> none  [the longest x2 15.9 us: on_device(): lax.all_to_all(product, 'fsdp', split_axis=0, concat_axis=0, tiled=True)]
  transfers between devices with their start and end apart: 8 -> 0, of which waited for: 7 -> 0; matrix products, arithmetic and copies ran while one was open for 5% -> 0% of each run, Pallas kernels for 0% -> 0%
where the time goes in v1:
time: 103 us; the launch traced here: 102 us
  Pallas kernels  88.3 us (86%)
  local copies, waits for them, and re-layouts  11.3 us (11%)
  other arithmetic  2.45 us (2%)
    pallas_call x1, Pallas kernels, on_device(): pl.pallas_call(kernel, out_shape=jax.ShapeDtypeStruct((8, D), f32), in_sp...  88.3 us
    unnamed x16, local copies, waits for them, and re-layouts  9.73 us

profile of v1, /device:TPU:1, one launch (start us, length us, event | category | flops | bytes accessed | tf_op | source)
XLA Modules:
  0.0 102.1 jit_solution(4704558348395708278)
XLA Ops:
  0.0 0.9 multiply_reduce_fusion
  0.9 0.1 rsqrt.12
  1.0 0.7 slice_convert_fusion.gain_ref
  1.7 0.7 convert_reduce_fusion
  2.5 0.8 copy.20.new_wk
  3.3 0.8 copy.21.new_wv
  4.0 0.8 reshape.23.xr_ref
  4.8 0.1 fusion.x0_ref
  4.9 1.2 %copy.19.new_wq = bf16[2,20,4096]{2,1,0:T(8,128)(2,1)S(1)} copy(bf16[2,20,4096]{2,0,1:T(2,128)(2,1)} %param.20) | data formatting | bytes 655360 | tf_op args[6]
  6.1 1.2 %copy.22.new_wo = bf16[2,20,4096]{2,1,0:T(8,128)(2,1)S(1)} copy(bf16[2,20,4096]{2,0,1:T(2,128)(2,1)} %param.23) | data formatting | bytes 655360 | tf_op args[9]
  7.2 0.0 copy-start
  7.3 1.3 %copy-done = bf16[2,2560,128]{2,1,0:T(8,128)(2,1)S(1)} copy-done((bf16[2,2560,128]{2,1,0:T(8,128)(2,1)S(1)}, bf16[2,2560,128]{2,1,0:T(8,128)(2,1)}, u32[]{:S(2)}) %copy-start) | copy-done | bytes 1310744
  8.6 0.0 copy-start.1
  8.6 1.3 %copy-done.1 = bf16[2,2560,128]{2,1,0:T(8,128)(2,1)S(1)} copy-done((bf16[2,2560,128]{2,1,0:T(8,128)(2,1)S(1)}, bf16[2,2560,128]{2,1,0:T(8,128)(2,1)}, u32[]{:S(2)}) %copy-start.1) | copy-done | bytes 1310744
  9.9 0.0 copy-start.2
  9.9 0.9 copy-done.2
  10.8 0.0 copy-start.3
  10.8 0.9 copy-done.3
  11.8 0.0 copy-start.4
  11.8 0.7 copy-done.4
  12.4 0.0 copy-start.5
  12.4 0.7 copy-done.5
  13.1 88.3 %shard_map.136 = f32[8,2560]{1,0:T(8,128)S(1)} custom-call(f32[8,2560]{1,0:T(8,128)S(1)} %fusion.x0_ref, f32[8,2560]{1,0:T(8,128)S(1)} %reshape.23.xr_ref, f32[1,2560]{1,0:T(1,128)S(1)} %slice_convert_fusion.gain_ref, s32[2]{0:T(128)S(1)} %copy-done.4, s32[4]{0:T(128)S(1)} %copy-done.5, bf16[2,2560,1024]{2,1,0:T(8,128)(2,1)} %old_wq.1, ...), custom_call_target="tpu_custom_call" | custom-call | tf_op jit(solution)/shard_map/pallas_call | solution.py:585
  101.4 0.7 reshape.24
  (1 shorter events, 0.0 us)
Async XLA Ops:
  7.2 1.3 %copy-start = (bf16[2,2560,128]{2,1,0:T(8,128)(2,1)S(1)}, bf16[2,2560,128]{2,1,0:T(8,128)(2,1)}, u32[]{:S(2)}) copy-start(bf16[2,2560,128]{2,1,0:T(8,128)(2,1)} %old_wk.1) | copy-start | bytes 3932164
  8.6 1.3 %copy-start.1 = (bf16[2,2560,128]{2,1,0:T(8,128)(2,1)S(1)}, bf16[2,2560,128]{2,1,0:T(8,128)(2,1)}, u32[]{:S(2)}) copy-start(bf16[2,2560,128]{2,1,0:T(8,128)(2,1)} %old_wv.1) | copy-start | bytes 3932164
  9.9 0.9 copy-start.2
  10.8 0.9 copy-start.3
  11.8 0.7 copy-start.4
  12.4 0.7 copy-start.5
